TPU v7x, 32 devices: a whole 2x2x4 slice. The times are simulated.
32 devices in a mesh: batch: 8 (over y, x, core), mp: 4 (over z).
Axes of the slice: x: 2, y: 2, z: 4, core: 2. Of those that a mesh axis runs over, the one named last changes fastest.
Arguments:
- residual: bfloat16 [8, 64, 8192], P('batch', None, 'mp'), may hold values from -6 to 6
- query_states: bfloat16 [8, 64, 4096], P('batch', None, 'mp')
- key_states: bfloat16 [8, 64, 512], P('batch')
- value_states: bfloat16 [8, 64, 512], P('batch'), may hold values from -6 to 6
- prompt_perm: int32 [8], replicated, may hold values from 0 to 7, each once
- ablated_heads: int32 [8], replicated, may hold values from 0 to 31, as said below
- out_weight: bfloat16 [4096, 8192], P('batch', 'mp'), may hold values from -0.09375 to 0.09375
- rms_gain: float32 [8192], P('mp'), may hold values from 0.1 to 1.9
- gate_weight: bfloat16 [8192, 14336], P('mp', 'batch'), may hold values from -0.0625 to 0.0625
- up_weight: bfloat16 [8192, 14336], P('mp', 'batch'), may hold values from -0.0625 to 0.0625
- down_weight: bfloat16 [14336, 8192], P('batch', 'mp'), may hold values from -0.046875 to 0.046875
Outputs:
- attn_out: bfloat16 [8, 64, 8192], P('batch', None, 'mp')
- mlp_out: bfloat16 [8, 64, 8192], P('batch', None, 'mp')
Inputs may be any that keep to these rules, and one draw needn't show every extreme that they name: `prompt_perm`: each prompt index appears exactly once. `ablated_heads`: 8 different head indices in any order, one of them 32 - 1.
All inputs are finite; a program needn't handle non-finite values.
Results may differ from a plain program's by a relative error of at most 0.035.
Values may be sent and summed in bfloat16 or wider, within the bound.
A program may use at most 128 MiB of HBM per device.

v0:
```python
import math
import jax
import jax.numpy as jnp
from jax import lax
from jax.sharding import PartitionSpec as P

D = 8192
HEADS = 32
KV = 4
HD = 128
ABLATED = 8


def local_heads(query_states, key_states, value_states):
    prompts_here, length, columns = query_states.shape
    head_count = columns // HD
    first_head = lax.axis_index("mp") * head_count
    owners = (first_head + jnp.arange(head_count)) // (HEADS // KV)
    query_four = query_states.reshape(prompts_here, length, head_count, HD)
    key_four = jnp.take(key_states.reshape(prompts_here, length, KV, HD), owners, axis=2)
    value_four = jnp.take(value_states.reshape(prompts_here, length, KV, HD), owners, axis=2)
    scores = jnp.einsum(
        "pshd,pthd->phst", query_four, key_four, preferred_element_type=jnp.float32
    ) / math.sqrt(HD)
    positions = jnp.arange(length)
    causal = positions[:, None] >= positions[None, :]
    scores = jnp.where(causal, scores, -1e30)
    highest = jnp.max(scores, axis=-1, keepdims=True)
    weights = jnp.exp(scores - highest)
    probability = (weights / jnp.sum(weights, axis=-1, keepdims=True)).astype(jnp.bfloat16)
    mixed_heads = jnp.einsum(
        "phst,pthd->pshd", probability, value_four, preferred_element_type=jnp.float32
    )
    return mixed_heads.astype(jnp.bfloat16).reshape(prompts_here, length, head_count * HD)


def body(
    residual,
    query_states,
    key_states,
    value_states,
    prompt_perm,
    ablated_heads,
    out_weight,
    rms_gain,
    gate_weight,
    up_weight,
    down_weight,
):
    prompts_here, length, model_cols = residual.shape
    local_rows = prompts_here * length
    head_block = local_heads(query_states, key_states, value_states)
    all_heads = lax.all_gather(head_block, "mp", axis=2, tiled=True)
    batch_index = lax.axis_index("batch")
    sources = jnp.take(prompt_perm, batch_index * prompts_here + jnp.arange(prompts_here))
    stacked = all_heads.reshape(prompts_here, length, HEADS, HD)
    picked_cols = jnp.take(stacked, ablated_heads, axis=2).reshape(
        prompts_here, length * ABLATED * HD
    )
    block_rows = lax.all_gather(picked_cols, "batch", axis=0, tiled=True)
    selector = (sources[:, None] == jnp.arange(block_rows.shape[0])[None, :]).astype(jnp.bfloat16)
    picked = jnp.dot(selector, block_rows, preferred_element_type=jnp.float32)
    picked_four = picked.astype(jnp.bfloat16).reshape(prompts_here, length, ABLATED, HD)
    placing = (jnp.arange(HEADS)[:, None] == ablated_heads[None, :]).astype(jnp.bfloat16)
    placed = jnp.einsum(
        "psad,ga->psgd", picked_four, placing, preferred_element_type=jnp.float32
    ).astype(jnp.bfloat16)
    chosen = jnp.any(jnp.arange(HEADS)[:, None] == ablated_heads[None, :], axis=1)
    mixed_heads = jnp.where(chosen[None, None, :, None], placed, stacked).reshape(
        local_rows, HEADS * HD
    )
    attn_float = jnp.dot(
        mixed_heads,
        lax.all_gather(out_weight, "batch", axis=0, tiled=True),
        preferred_element_type=jnp.float32,
    )
    attn_out = attn_float.astype(jnp.bfloat16)
    hidden_state = residual.reshape(local_rows, model_cols).astype(jnp.float32) + attn_float
    squares = lax.psum(jnp.sum(hidden_state * hidden_state, axis=1), "mp")
    inverse = lax.rsqrt(squares / D + 1e-05)
    normed = (hidden_state * inverse[:, None] * rms_gain[None, :]).astype(jnp.bfloat16)
    block_rows = lax.all_gather(normed, "batch", axis=0, tiled=True)
    gate_part = jnp.dot(block_rows, gate_weight, preferred_element_type=jnp.float32)
    up_part = jnp.dot(block_rows, up_weight, preferred_element_type=jnp.float32)
    partial_value = jnp.concatenate([gate_part, up_part], axis=1)
    slice_width = gate_weight.shape[1]
    summed = lax.psum(partial_value.astype(jnp.bfloat16), "mp").astype(jnp.float32)
    hidden = (jax.nn.silu(summed[:, :slice_width]) * summed[:, slice_width:]).astype(jnp.bfloat16)
    block_rows = hidden
    mlp_float = lax.psum_scatter(
        jnp.dot(block_rows, down_weight, preferred_element_type=jnp.float32).astype(jnp.bfloat16),
        "batch",
        scatter_dimension=0,
        tiled=True,
    )
    return (
        attn_out.reshape(prompts_here, length, model_cols),
        mlp_float.reshape(prompts_here, length, model_cols),
    )


def solution(mesh):
    placed = (
        P("batch", None, "mp"),
        P("batch", None, "mp"),
        P("batch", None, None),
        P("batch", None, None),
        P(),
        P(),
        P("batch", "mp"),
        P("mp"),
        P("mp", "batch"),
        P("mp", "batch"),
        P("batch", "mp"),
    )
    return jax.shard_map(
        body,
        mesh=mesh,
        in_specs=placed,
        out_specs=(P("batch", None, "mp"), P("batch", None, "mp")),
        check_vma=False,
    )
```

profile of v0, /device:TPU:0, one launch (start us, length us, event | category | flops | bytes accessed | tf_op | source)
XLA Modules:
  0.0 413.6 jit_solution(484651136919230348)
XLA Ops:
  7.3 0.7 compare_select_fusion.1
  7.9 0.7 compare_and_fusion.1
  8.6 0.9 copy.37
  9.6 0.6 gather_fusion.2
  10.5 0.9 bitcast_bitcast_fusion.1
  12.3 17.4 %all_gather.12 = bf16[1,64,4096]{2,1,0:T(8,128)(2,1)S(1)} all-gather(bf16[1,64,1024]{2,1,0:T(8,128)(2,1)S(1)} %bitcast.109), channel_id=1, replica_groups=mesh['batch'=8,'mp'=4] {'mp'}, dimensions={2}, use_global_device_ids=true | all-gather | bytes 655360 | tf_op jit(solution)/shard_map/all_gather | solution.py:53
  30.0 0.6 gather_fusion
  30.7 0.8 reshape.200
  31.6 0.7 all-gather.5.cloned.1.call-update
  32.3 0.6 dynamic-slice.2
  33.6 27.7 %all-gather.9.cloned.1.call-done = bf16[8,1,65536]{2,1,0:T(2,128)(2,1)} async-done(((bf16[1,1,65536]{2,1,0:T(2,128)(2,1)}), bf16[8,1,65536]{2,1,0:T(2,128)(2,1)}) %all-gather.9.cloned.1.call-update) | async-done | bytes 1048592 | tf_op jit(solution)/shard_map/all_gather | solution.py:60
  61.3 2.9 fusion.11
  64.6 88.5 %all-gather.5.cloned.1.call-done = bf16[4096,2048]{1,0:T(8,128)(2,1)} async-done(((bf16[512,2048]{1,0:T(8,128)(2,1)}), bf16[4096,2048]{1,0:T(8,128)(2,1)}) %all-gather.5.cloned.1.call-update) | async-done | bytes 16777232 | tf_op jit(solution)/shard_map/all_gather | solution.py:74
  153.1 8.9 %multiply_reduce_fusion = (f32[64]{0:T(128)S(1)}, f32[64,2048]{1,0:T(8,128)S(1)}) fusion(bf16[1,64,2048]{2,1,0:T(8,128)(2,1)S(1)} %copy-done.2, bf16[4096,2048]{1,0:T(8,128)(2,1)} %all-gather.5.cloned.1.call-done, bf16[8,8,32,128]{3,2,1,0:T(8,128)(2,1)S(1)} %bitcast.106), kind=kOutput, calls=%fused_computation.29 | convolution fusion | flops 1074266112 | bytes 18088192 | tf_op jit(solution)/shard_map/dot_general | solution.py:72
  162.0 11.7 %psum.14 = f32[64]{0:T(128)S(1)} all-reduce(f32[64]{0:T(128)S(1)} %get-tuple-element.16), channel_id=1, replica_groups=mesh['batch'=8,'mp'=4] {'mp'}, use_global_device_ids=true, to_apply=%region_4.6 | all-reduce | flops 64 | bytes 512 | tf_op jit(solution)/shard_map/psum | solution.py:79
  173.7 0.8 multiply_convert_fusion
  174.8 25.1 %all-gather.7.cloned.1.call-done = bf16[512,2048]{1,0:T(8,128)(2,1)} async-done(((bf16[64,2048]{1,0:T(8,128)(2,1)}), bf16[512,2048]{1,0:T(8,128)(2,1)}) %all-gather.7.cloned.1.call-update) | async-done | bytes 2097168 | tf_op jit(solution)/shard_map/all_gather | solution.py:82
  199.9 7.8 %convolution_convert_fusion.1 = bf16[512,1792]{1,0:T(8,128)(2,1)S(1)} fusion(bf16[512,2048]{1,0:T(8,128)(2,1)} %all-gather.7.cloned.1.call-done, bf16[2048,1792]{1,0:T(8,128)(2,1)} %param.22), kind=kOutput, calls=%fused_computation.8 | convolution fusion | flops 3759013888 | bytes 11272192 | tf_op jit(solution)/shard_map/dot_general | solution.py:84
  207.7 7.0 %convolution_convert_fusion.2 = bf16[512,1792]{1,0:T(8,128)(2,1)S(1)} fusion(bf16[512,2048]{1,0:T(8,128)(2,1)S(1)} %copy-done.5, bf16[2048,1792]{1,0:T(8,128)(2,1)} %param.21), kind=kOutput, calls=%fused_computation.9 | convolution fusion | flops 3759013888 | bytes 11272192 | tf_op jit(solution)/shard_map/dot_general | solution.py:83
  214.7 2.1 pad_maximum_fusion
  216.9 138.2 %all-reduce.2.cloned.1.call-done = bf16[512,3584]{1,0:T(8,128)(2,1)} async-done(((bf16[512,3584]{1,0:T(8,128)(2,1)}), bf16[512,3584]{1,0:T(8,128)(2,1)}) %all-reduce.2.cloned.1.call-update) | async-done | bytes 3670032 | tf_op jit(solution)/shard_map/psum | solution.py:87
  355.1 3.0 convert_element_type.62
  358.1 8.5 %convolution_convert_fusion = bf16[512,2048]{1,0:T(8,128)(2,1)} fusion(bf16[1792,2048]{1,0:T(8,128)(2,1)} %param.23, f32[512,3584]{1,0:T(8,128)S(1)} %convert_element_type.62), kind=kOutput, calls=%fused_computation.7 | convolution fusion | flops 3764649984 | bytes 16777216 | tf_op jit(solution)/shard_map/dot_general | solution.py:91
  366.7 40.4 %reduce-scatter.2.cloned.1.call-done = bf16[64,2048]{1,0:T(8,128)(2,1)} async-done(((bf16[512,2048]{1,0:T(8,128)(2,1)}), bf16[64,2048]{1,0:T(8,128)(2,1)}) %reduce-scatter.2.cloned.1.call-update) | async-done | bytes 262160 | tf_op jit(solution)/shard_map/reduce_scatter | solution.py:90
  (41 shorter events, 2.7 us)
Async XLA Ops:
  7.2 1.5 copy-start
  7.2 54.1 %all-gather.9.cloned.1.call-start = ((), (), s32[]{:S(2)}) async-start(), calls=%async_computation.5 | async-start | bytes 2359296 | tf_op jit(solution)/shard_map/all_gather | solution.py:60
  11.9 20.4 %copy-start.6 = (s32[8]{0:T(128)S(1)}, s32[8]{0:T(128)}, u32[]{:S(2)}) copy-start(s32[8]{0:T(128)} %param.17) | copy-start | bytes 100
  12.0 21.6 %copy-start.4 = (s32[8]{0:T(128)S(1)}, s32[8]{0:T(128)}, u32[]{:S(2)}) copy-start(s32[8]{0:T(128)} %param.18) | copy-start | bytes 100
  29.7 123.4 %copy-start.2 = (bf16[1,64,2048]{2,1,0:T(8,128)(2,1)S(1)}, bf16[1,64,2048]{2,1,0:T(8,128)(2,1)}, u32[]{:S(2)}) copy-start(bf16[1,64,2048]{2,1,0:T(8,128)(2,1)} %param.13) | copy-start | bytes 786436
  31.5 121.6 %all-gather.5.cloned.1.call-start = ((), (), s32[]{:S(2)}) async-start(), calls=%async_computation.1 | async-start | bytes 18874368 | tf_op jit(solution)/shard_map/all_gather | solution.py:74
  32.3 167.6 %all-gather.7.cloned.1.call-start = ((), (), s32[]{:S(2)}) async-start(), calls=%async_computation.2 | async-start | bytes 2359296 | tf_op jit(solution)/shard_map/all_gather | solution.py:82
  153.1 20.6 %copy-start.3 = (f32[2048]{0:T(1024)S(1)}, f32[2048]{0:T(1024)}, u32[]{:S(2)}) copy-start(f32[2048]{0:T(1024)} %param.20) | copy-start | bytes 24580
  174.6 180.5 %all-reduce.2.cloned.1.call-start = ((), (), s32[]{:S(2)}) async-start(), calls=%async_computation.3 | async-start | bytes 7340032 | tf_op jit(solution)/shard_map/psum | solution.py:87
  199.9 7.8 %copy-start.5 = (bf16[512,2048]{1,0:T(8,128)(2,1)S(1)}, bf16[512,2048]{1,0:T(8,128)(2,1)}, u32[]{:S(2)}) copy-start(bf16[512,2048]{1,0:T(8,128)(2,1)} %all-gather.7.cloned.1.call-done) | copy-start | bytes 6291460
  216.9 190.2 %reduce-scatter.2.cloned.1.call-start = ((), (), s32[]{:S(2)}) async-start(), calls=%async_computation.4 | async-start | bytes 2359296 | tf_op jit(solution)/shard_map/reduce_scatter | solution.py:90
  358.1 49.0 %copy-start.1 = (bf16[1,64,512]{2,1,0:T(8,128)(2,1)S(1)}, bf16[1,64,512]{2,1,0:T(8,128)(2,1)}, u32[]{:S(2)}) copy-start(bf16[1,64,512]{2,1,0:T(8,128)(2,1)} %param.15) | copy-start | bytes 196612
Sparse Core Ops, SparseCore 0:
  31.6 29.6 all-gather.8
  63.2 89.8 all-gather.4
  174.7 25.1 all-gather.6
  217.0 138.0 all-reduce.1
  366.8 40.2 reduce-scatter.1
where the time goes:
time: 414 us
  waiting for transfers between devices  321 us (78%)
  matrix products  36.1 us (9%)
  blocking collectives  29.1 us (7%)
  between operations  14.6 us (4%)
  other arithmetic  7.56 us (2%)
  local copies, waits for them, and re-layouts  5.31 us (1%)
    psum x1, waiting for transfers between devices, body(): lax.psum(partial_value.astype(jnp.bfloat16), 'mp').astype(jnp.float32)  138 us
    all_gather x1, waiting for transfers between devices, body(): lax.all_gather(out_weight, 'batch', axis=0, tiled=True)  88.5 us
    reduce_scatter x1, waiting for transfers between devices, body(): lax.psum_scatter(jnp.dot(block_rows, down_weight, preferred_element_type=...  40.4 us
    all_gather x1, waiting for transfers between devices, body(): block_rows = lax.all_gather(picked_cols, 'batch', axis=0, tiled=True)  27.7 us
    all_gather x1, waiting for transfers between devices, body(): block_rows = lax.all_gather(normed, 'batch', axis=0, tiled=True)  25.1 us
    all_gather x1, blocking collectives, body(): all_heads = lax.all_gather(head_block, 'mp', axis=2, tiled=True)  17.4 us
    psum x1, blocking collectives, body(): squares = lax.psum(jnp.sum(hidden_state * hidden_state, axis=1), 'mp')  11.7 us
    dot_general x1, matrix products, body(): jnp.dot(mixed_heads, lax.all_gather(out_weight, 'batch', axis=0, tiled=Tr...  8.92 us
  transfers between devices with their start and end apart: 5, of which 5 were waited for; matrix products, arithmetic and copies ran while one was open for 1% of the time, Pallas kernels for 0%

commit v1 on v0

--- a/solution.py
+++ b/solution.py
@@ -84,7 +84,9 @@
     up_part = jnp.dot(block_rows, up_weight, preferred_element_type=jnp.float32)
     partial_value = jnp.concatenate([gate_part, up_part], axis=1)
     slice_width = gate_weight.shape[1]
-    summed = lax.psum(partial_value.astype(jnp.bfloat16), "mp").astype(jnp.float32)
+    summed = jnp.sum(lax.all_gather(partial_value.astype(jnp.bfloat16), "mp"), axis=0).astype(
+        jnp.float32
+    )
     hidden = (jax.nn.silu(summed[:, :slice_width]) * summed[:, slice_width:]).astype(jnp.bfloat16)
     block_rows = hidden
     mlp_float = lax.psum_scatter(

time: 414 us -> 538 us (1.30)
  waiting for transfers between devices: 321 us -> 434 us
  other arithmetic: 7.56 us -> 18.2 us
    all_gather x0 -> x1, waiting for transfers between devices: none -> 253 us  [body(): lax.all_gather(partial_value.astype(jnp.bfloat16), 'mp')]
    psum x1 -> x0, waiting for transfers between devices: 138 us -> none  [body(): lax.psum(partial_value.astype(jnp.bfloat16), 'mp').astype(jnp.float32)]
    reduce_sum x0 -> x1, other arithmetic: none -> 10.7 us  [body(): jnp.sum(lax.all_gather(partial_value.astype(jnp.bfloat16), 'mp'), axis=0)]
where the time goes in v1:
time: 538 us
  waiting for transfers between devices  434 us (81%)
  matrix products  36.1 us (7%)
  blocking collectives  29.1 us (5%)
  other arithmetic  18.2 us (3%)
  between operations  14.6 us (3%)
    all_gather x1, waiting for transfers between devices, body(): lax.all_gather(partial_value.astype(jnp.bfloat16), 'mp')  253 us
    all_gather x1, waiting for transfers between devices, body(): lax.all_gather(out_weight, 'batch', axis=0, tiled=True)  88.5 us
    reduce_scatter x1, waiting for transfers between devices, body(): lax.psum_scatter(jnp.dot(block_rows, down_weight, preferred_element_type=...  39.6 us
    all_gather x1, waiting for transfers between devices, body(): block_rows = lax.all_gather(picked_cols, 'batch', axis=0, tiled=True)  27.7 us
    all_gather x1, waiting for transfers between devices, body(): block_rows = lax.all_gather(normed, 'batch', axis=0, tiled=True)  25.1 us
    all_gather x1, blocking collectives, body(): all_heads = lax.all_gather(head_block, 'mp', axis=2, tiled=True)  17.4 us
    psum x1, blocking collectives, body(): squares = lax.psum(jnp.sum(hidden_state * hidden_state, axis=1), 'mp')  11.7 us
  transfers between devices with their start and end apart: 5, of which 5 were waited for; matrix products, arithmetic and copies ran while one was open for 1% of the time, Pallas kernels for 0%

profile of v1, /device:TPU:0, one launch (start us, length us, event | category | flops | bytes accessed | tf_op | source)
XLA Modules:
  0.0 537.8 jit_solution(1538323809379130294)
XLA Ops:
  7.3 0.7 compare_select_fusion.1
  7.9 0.7 compare_and_fusion.1
  8.6 0.9 copy.37
  9.6 0.6 gather_fusion.2
  10.5 0.9 bitcast_bitcast_fusion.1
  12.3 17.4 %all_gather.16 = bf16[1,64,4096]{2,1,0:T(8,128)(2,1)S(1)} all-gather(bf16[1,64,1024]{2,1,0:T(8,128)(2,1)S(1)} %bitcast.113), channel_id=1, replica_groups=mesh['batch'=8,'mp'=4] {'mp'}, dimensions={2}, use_global_device_ids=true | all-gather | bytes 655360 | tf_op jit(solution)/shard_map/all_gather | solution.py:53
  30.7 0.8 reshape.231
  31.6 0.7 all-gather.6.cloned.1.call-update
  32.3 0.6 dynamic-slice.2
  33.6 27.7 %all-gather.12.cloned.1.call-done = bf16[8,1,65536]{2,1,0:T(2,128)(2,1)} async-done(((bf16[1,1,65536]{2,1,0:T(2,128)(2,1)}), bf16[8,1,65536]{2,1,0:T(2,128)(2,1)}) %all-gather.12.cloned.1.call-update) | async-done | bytes 1048592 | tf_op jit(solution)/shard_map/all_gather | solution.py:60
  61.3 2.9 fusion.13
  64.6 88.5 %all-gather.6.cloned.1.call-done = bf16[4096,2048]{1,0:T(8,128)(2,1)} async-done(((bf16[512,2048]{1,0:T(8,128)(2,1)}), bf16[4096,2048]{1,0:T(8,128)(2,1)}) %all-gather.6.cloned.1.call-update) | async-done | bytes 16777232 | tf_op jit(solution)/shard_map/all_gather | solution.py:74
  153.1 8.9 %multiply_reduce_fusion = (f32[64]{0:T(128)S(1)}, f32[64,2048]{1,0:T(8,128)S(1)}) fusion(bf16[1,64,2048]{2,1,0:T(8,128)(2,1)S(1)} %copy-done.2, bf16[4096,2048]{1,0:T(8,128)(2,1)} %all-gather.6.cloned.1.call-done, bf16[8,8,32,128]{3,2,1,0:T(8,128)(2,1)S(1)} %bitcast.110), kind=kOutput, calls=%fused_computation.31 | convolution fusion | flops 1074266112 | bytes 18088192 | tf_op jit(solution)/shard_map/dot_general | solution.py:72
  162.0 11.7 %psum.7 = f32[64]{0:T(128)S(1)} all-reduce(f32[64]{0:T(128)S(1)} %get-tuple-element.16), channel_id=1, replica_groups=mesh['batch'=8,'mp'=4] {'mp'}, use_global_device_ids=true, to_apply=%region_4.6 | all-reduce | flops 64 | bytes 512 | tf_op jit(solution)/shard_map/psum | solution.py:79
  173.7 0.8 multiply_convert_fusion
  174.8 25.1 %all-gather.8.cloned.1.call-done = bf16[512,2048]{1,0:T(8,128)(2,1)} async-done(((bf16[64,2048]{1,0:T(8,128)(2,1)}), bf16[512,2048]{1,0:T(8,128)(2,1)}) %all-gather.8.cloned.1.call-update) | async-done | bytes 2097168 | tf_op jit(solution)/shard_map/all_gather | solution.py:82
  199.9 7.8 %fusion.2 = bf16[1,512,1792]{2,1,0:T(8,128)(2,1)S(1)} fusion(bf16[512,2048]{1,0:T(8,128)(2,1)} %all-gather.8.cloned.1.call-done, bf16[2048,1792]{1,0:T(8,128)(2,1)} %param.21), kind=kOutput, calls=%fused_computation.10 | convolution fusion | flops 3759013888 | bytes 11272192 | tf_op jit(solution)/shard_map/dot_general | solution.py:83
  207.7 7.0 %fusion.3 = bf16[1,512,1792]{2,1,0:T(8,128)(2,1)S(1)} fusion(bf16[512,2048]{1,0:T(8,128)(2,1)S(1)} %copy-done.5, bf16[2048,1792]{1,0:T(8,128)(2,1)} %param.22), kind=kOutput, calls=%fused_computation.11 | convolution fusion | flops 3759013888 | bytes 11272192 | tf_op jit(solution)/shard_map/dot_general | solution.py:84
  214.7 2.1 pad_maximum_fusion
  216.9 252.6 %all-gather.10.cloned.1.call-done = bf16[4,512,3584]{2,1,0:T(8,128)(2,1)} async-done(((bf16[1,512,3584]{2,1,0:T(8,128)(2,1)}), bf16[4,512,3584]{2,1,0:T(8,128)(2,1)}) %all-gather.10.cloned.1.call-update) | async-done | bytes 14680080 | tf_op jit(solution)/shard_map/all_gather | solution.py:87
  469.5 10.7 %reduce_sum.32 = bf16[512,3584]{1,0:T(8,128)(2,1)} reduce(bf16[4,512,3584]{2,1,0:T(8,128)(2,1)} %all-gather.10.cloned.1.call-done, bf16[]{:T(256)} %constant.87.clone.1), dimensions={0}, to_apply=%region_5.7 | reduce | flops 5505024 | bytes 18350082 | tf_op jit(solution)/shard_map/reduce_sum | solution.py:87
  480.1 3.0 convert_element_type.71
  483.2 8.5 %convolution_convert_fusion = bf16[512,2048]{1,0:T(8,128)(2,1)} fusion(bf16[1792,2048]{1,0:T(8,128)(2,1)} %param.23, f32[512,3584]{1,0:T(8,128)S(1)} %convert_element_type.71), kind=kOutput, calls=%fused_computation.7 | convolution fusion | flops 3764649984 | bytes 16777216 | tf_op jit(solution)/shard_map/dot_general | solution.py:93
  491.7 39.6 %reduce-scatter.2.cloned.1.call-done = bf16[64,2048]{1,0:T(8,128)(2,1)} async-done(((bf16[512,2048]{1,0:T(8,128)(2,1)}), bf16[64,2048]{1,0:T(8,128)(2,1)}) %reduce-scatter.2.cloned.1.call-update) | async-done | bytes 262160 | tf_op jit(solution)/shard_map/reduce_scatter | solution.py:92
  (42 shorter events, 3.3 us)
Async XLA Ops:
  7.2 1.5 copy-start
  7.2 54.1 %all-gather.12.cloned.1.call-start = ((), (), s32[]{:S(2)}) async-start(), calls=%async_computation.5 | async-start | bytes 2359296 | tf_op jit(solution)/shard_map/all_gather | solution.py:60
  11.9 20.4 %copy-start.6 = (s32[8]{0:T(128)S(1)}, s32[8]{0:T(128)}, u32[]{:S(2)}) copy-start(s32[8]{0:T(128)} %param.17) | copy-start | bytes 100
  12.0 21.6 %copy-start.4 = (s32[8]{0:T(128)S(1)}, s32[8]{0:T(128)}, u32[]{:S(2)}) copy-start(s32[8]{0:T(128)} %param.18) | copy-start | bytes 100
  29.7 123.4 %copy-start.2 = (bf16[1,64,2048]{2,1,0:T(8,128)(2,1)S(1)}, bf16[1,64,2048]{2,1,0:T(8,128)(2,1)}, u32[]{:S(2)}) copy-start(bf16[1,64,2048]{2,1,0:T(8,128)(2,1)} %param.13) | copy-start | bytes 786436
  31.5 121.6 %all-gather.6.cloned.1.call-start = ((), (), s32[]{:S(2)}) async-start(), calls=%async_computation.1 | async-start | bytes 18874368 | tf_op jit(solution)/shard_map/all_gather | solution.py:74
  32.3 167.6 %all-gather.8.cloned.1.call-start = ((), (), s32[]{:S(2)}) async-start(), calls=%async_computation.2 | async-start | bytes 2359296 | tf_op jit(solution)/shard_map/all_gather | solution.py:82
  153.1 20.6 %copy-start.3 = (f32[2048]{0:T(1024)S(1)}, f32[2048]{0:T(1024)}, u32[]{:S(2)}) copy-start(f32[2048]{0:T(1024)} %param.20) | copy-start | bytes 24580
  174.6 294.9 %all-gather.10.cloned.1.call-start = ((), (), s32[]{:S(2)}) async-start(), calls=%async_computation.3 | async-start | bytes 18350080 | tf_op jit(solution)/shard_map/all_gather | solution.py:87
  199.9 7.8 %copy-start.5 = (bf16[512,2048]{1,0:T(8,128)(2,1)S(1)}, bf16[512,2048]{1,0:T(8,128)(2,1)}, u32[]{:S(2)}) copy-start(bf16[512,2048]{1,0:T(8,128)(2,1)} %all-gather.8.cloned.1.call-done) | copy-start | bytes 6291460
  216.8 314.5 %reduce-scatter.2.cloned.1.call-start = ((), (), s32[]{:S(2)}) async-start(), calls=%async_computation.4 | async-start | bytes 2359296 | tf_op jit(solution)/shard_map/reduce_scatter | solution.py:92
  483.1 48.2 %copy-start.1 = (bf16[1,64,512]{2,1,0:T(8,128)(2,1)S(1)}, bf16[1,64,512]{2,1,0:T(8,128)(2,1)}, u32[]{:S(2)}) copy-start(bf16[1,64,512]{2,1,0:T(8,128)(2,1)} %param.15) | copy-start | bytes 196612
Sparse Core Ops, SparseCore 0:
  31.6 29.6 all-gather.11
  63.2 89.8 all-gather.5
  174.7 25.1 all-gather.7
  217.0 252.4 all-gather.9
  491.8 39.4 reduce-scatter.1
